TPU v7x, 32 devices: a whole 2x2x4 slice. The times are simulated.
32 devices in a mesh: pipe: 4 (over z), expert: 4 (over x, core), tensor: 2 (over y).
Axes of the slice: x: 2, y: 2, z: 4, core: 2. Of those that a mesh axis runs over, the one named last changes fastest.
Arguments:
- acts: bfloat16 [4, 4, 256, 1792], P('pipe', 'expert'), may hold values from -6 to 6
- hidden_grad: bfloat16 [4, 2, 256, 1024], P('pipe', None, None, 'tensor'), may hold values from -0.5 to 0.5
- counts: int32 [4, 2, 2], P('pipe'), may hold values from 32 to 128, as said below
- momentum: bfloat16 [4, 4, 1792, 1024], P('pipe', 'expert', 'tensor'), may hold values from -6 to 6
- act_grad: bfloat16 [4, 256, 7168], P('pipe', 'expert', 'tensor'), may hold values from -6 to 6
Outputs:
- new_momentum: bfloat16 [4, 4, 1792, 1024], P('pipe', 'expert', 'tensor')
- gram_rows: float32 [4, 4, 256, 1024], P('pipe', 'expert', 'tensor')
- received: bfloat16 [4, 256, 7168], P('pipe', 'expert', 'tensor')
Inputs may be any that keep to these rules, and one draw needn't show every extreme that they name: `counts`: in every section and expert, at least one micro-batch fills its block.
All inputs are finite; a program needn't handle non-finite values.
Results may differ from a plain program's by a relative error of at most 0.0065.
Values may be sent and summed in bfloat16 or wider, within the bound.
A program may use at most 64 MiB of HBM per device.

v0:
```python
import jax
import jax.numpy as jnp
from jax import lax
from jax.sharding import PartitionSpec as P

D = 3584
PANEL = 512


momentum_decay = 0.9


def partner(block, axis, distance):
    count = lax.axis_size(axis)
    route = []
    for low in range(count):
        high = low | 1 << distance
        if high != low and high < count:
            route += [(low, high), (high, low)]
    return lax.ppermute(block, axis, route)


def from_behind(array, axis, by):
    count = lax.axis_size(axis)
    pairs = [(i, i + by) for i in range(count) if 0 <= i + by < count]
    return lax.ppermute(array, axis, pairs)


def contract(left, right):
    return lax.dot_general(
        left, right, (((0,), (0,)), ((), ())), preferred_element_type=jnp.float32
    )


def on_device(acts, hidden_grad, counts, momentum, act_grad):
    features = acts[0, 0]
    expert_rank = lax.axis_index("expert")
    pair_index = expert_rank // 2
    half_index = expert_rank % 2
    gradients = lax.dynamic_index_in_dim(hidden_grad[0], pair_index, 0, keepdims=False)
    counts_row = lax.dynamic_index_in_dim(counts[0], pair_index, 0, keepdims=False)
    row_count = features.shape[0]
    micro_count = counts_row.shape[0]
    block_rows = row_count // micro_count
    live_rows = (counts_row[:, None] > lax.iota(jnp.int32, block_rows)[None, :]).reshape(row_count)
    masked = jnp.where(live_rows[:, None], gradients, jnp.zeros_like(gradients))
    slice_grad = contract(features, masked).astype(jnp.bfloat16)
    grad_w = lax.all_to_all(slice_grad, "tensor", split_axis=0, concat_axis=1, tiled=True)
    new_momentum = (
        momentum_decay * momentum[0, 0].astype(jnp.float32) + grad_w.astype(jnp.float32)
    ).astype(jnp.bfloat16)
    share_rows = PANEL // lax.axis_size("tensor")
    columns = lax.slice_in_dim(new_momentum, 0, share_rows * lax.axis_size("tensor"), axis=1)
    partial_panel = lax.psum_scatter(
        contract(columns, new_momentum).astype(jnp.bfloat16),
        "tensor",
        scatter_dimension=0,
        tiled=True,
    ).astype(jnp.float32)
    quarter = share_rows // 2
    own_rows = lax.dynamic_slice_in_dim(partial_panel, half_index * quarter, quarter, 0)
    other_rows = lax.dynamic_slice_in_dim(partial_panel, (1 - half_index) * quarter, quarter, 0)
    partner_rows = partner(other_rows.astype(jnp.bfloat16), "expert", 0).astype(other_rows.dtype)
    gram_block = (own_rows + partner_rows) / D
    received = from_behind(act_grad, "pipe", -1)
    return (new_momentum[None, None], gram_block[None, None], received)


def solution(mesh):
    return jax.shard_map(
        on_device,
        mesh=mesh,
        in_specs=(
            P("pipe", "expert", None, None),
            P("pipe", None, None, "tensor"),
            P("pipe", None, None),
            P("pipe", "expert", "tensor", None),
            P("pipe", "expert", "tensor"),
        ),
        out_specs=(
            P("pipe", "expert", "tensor", None),
            P("pipe", "expert", "tensor", None),
            P("pipe", "expert", "tensor"),
        ),
        check_vma=False,
    )
```

profile of v0, /device:TPU:0, one launch (start us, length us, event | category | flops | bytes accessed | tf_op | source)
XLA Modules:
  0.0 83.2 jit_solution(5603996065570937611)
XLA Ops:
  7.2 0.0 copy-start
  7.2 0.0 reduce-scatter.2.cloned.1.call-start
  7.2 0.8 fusion.9
  8.0 0.1 compare_bitcast_fusion
  8.1 0.3 copy-done
  8.4 1.7 %convolution_convert_fusion = bf16[512,1792]{1,0:T(8,128)(2,1)S(1)} fusion(bf16[1,1,256,1792]{3,2,1,0:T(8,128)(2,1)S(1)} %copy-done, bf16[1,2,256,512]{3,2,1,0:T(8,128)(2,1)} %param.6, s32[]{:T(128)S(6)} %select_n.31, pred[256]{0:T(512)(128)(4,1)S(1)} %compare_bitcast_fusion), kind=kOutput, calls=%fused_computation.4 | convolution fusion | flops 470810624 | bytes 3014916 | tf_op jit(solution)/shard_map/dot_general | solution.py:30
  10.1 0.1 copy.15
  10.2 26.1 %all_to_all.13 = bf16[2,896,512]{1,2,0:T(8,128)(2,1)S(1)} all-to-all(bf16[2,896,512]{1,2,0:T(8,128)(2,1)S(1)} %bitcast.29), channel_id=1, replica_groups=mesh['pipe'=4,'expert'=4,'tensor'=2] {'tensor'}, dimensions={0} | all-to-all | bytes 3670016 | tf_op jit(solution)/shard_map/all_to_all | solution.py:48
  36.3 2.0 %convert_element_type.67 = f32[2,896,512]{1,2,0:T(8,128)} convert(bf16[2,896,512]{1,2,0:T(8,128)(2,1)S(1)} %all_to_all.13) | non-fusion elementwise | flops 917504 | bytes 5505024 | tf_op jit(solution)/shard_map/convert_element_type | solution.py:50
  38.3 5.2 %copy.12 = f32[896,1024]{1,0:T(8,128)} copy(f32[896,1024]{0,1:T(8,128)} %bitcast.27) | data formatting | bytes 7340032 | tf_op jit(solution)/shard_map/convert_element_type | solution.py:50
  43.5 0.0 copy-done.1
  43.5 2.7 %fusion = bf16[896,1024]{1,0:T(8,128)(2,1)S(1)} fusion(f32[896,1024]{1,0:T(8,128)} %copy.12, bf16[1,1,896,1024]{3,2,1,0:T(8,128)(2,1)S(1)} %copy-done.1), kind=kLoop, calls=%fused_computation.1 | loop fusion | flops 3670016 | bytes 7340032 | tf_op jit(solution)/shard_map/convert_element_type | solution.py:51
  46.2 2.3 %convolution_convert_fusion.1 = bf16[512,1024]{1,0:T(8,128)(2,1)} fusion(bf16[896,1024]{1,0:T(8,128)(2,1)S(1)} %fusion), kind=kOutput, calls=%fused_computation.6 | convolution fusion | flops 940048384 | bytes 3801088 | tf_op jit(solution)/shard_map/dot_general | solution.py:30
  48.5 0.0 reduce-scatter.2.cloned.1.call-update
  48.5 1.3 %collective-permute-start.1 = (bf16[1,64,3584]{2,1,0:T(8,128)(2,1)}, bf16[1,64,3584]{2,1,0:T(8,128)(2,1)S(1)}, u32[]{:S(2)}, u32[]{:S(2)}) collective-permute-start(bf16[1,64,3584]{2,1,0:T(8,128)(2,1)} %param.9), channel_id=1, source_target_pairs={{8,0},{16,8},{24,16},{9,1},{17,9},{25,17},{10,2},{18,10},{26,18},{... | collective-permute-start | bytes 1376264 | tf_op jit(solution)/shard_map/ppermute | solution.py:26
  49.8 12.2 %collective-permute-done.1 = bf16[1,64,3584]{2,1,0:T(8,128)(2,1)S(1)} collective-permute-done((bf16[1,64,3584]{2,1,0:T(8,128)(2,1)}, bf16[1,64,3584]{2,1,0:T(8,128)(2,1)S(1)}, u32[]{:S(2)}, u32[]{:S(2)}) %collective-permute-start.1) | collective-permute-done | bytes 458784 | tf_op jit(solution)/shard_map/ppermute | solution.py:26
  62.0 5.1 %copy.11 = f32[1,1,896,1024]{3,2,1,0:T(8,128)} copy(f32[1,1,896,1024]{2,3,1,0:T(8,128)} %bitcast.28) | data formatting | bytes 7340032 | tf_op jit(solution)/shard_map/convert_element_type | solution.py:50
  67.1 2.4 %reduce-scatter.2.cloned.1.call-done = bf16[256,1024]{1,0:T(8,128)(2,1)} async-done(((bf16[512,1024]{1,0:T(8,128)(2,1)}), bf16[256,1024]{1,0:T(8,128)(2,1)}) %reduce-scatter.2.cloned.1.call-update) | async-done | bytes 524304 | tf_op jit(solution)/shard_map/reduce_scatter | solution.py:54
  69.5 1.1 %convert_element_type.62 = f32[256,1024]{1,0:T(8,128)S(1)} convert(bf16[256,1024]{1,0:T(8,128)(2,1)} %reduce-scatter.2.cloned.1.call-done) | non-fusion elementwise | flops 262144 | bytes 1572864 | tf_op jit(solution)/shard_map/convert_element_type | solution.py:59
  70.7 0.1 collective-permute-start
  70.8 3.9 %add_convert_fusion = bf16[1,1,896,1024]{3,2,1,0:T(8,128)(2,1)} fusion(f32[1,1,896,1024]{3,2,1,0:T(8,128)} %copy.11, bf16[1,1,896,1024]{3,2,1,0:T(8,128)(2,1)S(1)} %copy-done.1), kind=kLoop, calls=%fused_computation.2 | loop fusion | flops 3670016 | bytes 7340032 | tf_op jit(solution)/shard_map/convert_element_type | solution.py:51
  74.7 0.0 collective-permute-done
  74.7 0.9 %multiply_bitcast_fusion = f32[1,1,128,1024]{3,2,1,0:T(8,128)} fusion(bf16[128,1024]{1,0:T(8,128)(2,1)S(1)} %collective-permute-done, f32[256,1024]{1,0:T(8,128)S(1)} %convert_element_type.62, s32[]{:T(128)S(6)} %select_n.35), kind=kLoop, calls=%fused_computation.9 | loop fusion | flops 393216 | bytes 1310724 | tf_op jit(solution)/shard_map/broadcast_in_dim | solution.py:66
  75.6 0.8 copy.17
  (2 shorter events, 0.0 us)
Async XLA Ops:
  7.2 1.2 %copy-start = (bf16[1,1,256,1792]{3,2,1,0:T(8,128)(2,1)S(1)}, bf16[1,1,256,1792]{3,2,1,0:T(8,128)(2,1)}, u32[]{:S(2)}) copy-start(bf16[1,1,256,1792]{3,2,1,0:T(8,128)(2,1)} %param.5) | copy-start | bytes 2752516
  7.2 62.3 %reduce-scatter.2.cloned.1.call-start = ((), (), s32[]{:S(2)}) async-start(), calls=%async_computation.2 | async-start | bytes 1572864 | tf_op jit(solution)/shard_map/reduce_scatter | solution.py:54
  38.3 5.2 %copy-start.1 = (bf16[1,1,896,1024]{3,2,1,0:T(8,128)(2,1)S(1)}, bf16[1,1,896,1024]{3,2,1,0:T(8,128)(2,1)}, u32[]{:S(2)}) copy-start(bf16[1,1,896,1024]{3,2,1,0:T(8,128)(2,1)} %param.8) | copy-start | bytes 5505028
  48.5 13.5 %collective-permute-start.1 = (bf16[1,64,3584]{2,1,0:T(8,128)(2,1)}, bf16[1,64,3584]{2,1,0:T(8,128)(2,1)S(1)}, u32[]{:S(2)}, u32[]{:S(2)}) collective-permute-start(bf16[1,64,3584]{2,1,0:T(8,128)(2,1)} %param.9), channel_id=1, source_target_pairs={{8,0},{16,8},{24,16},{9,1},{17,9},{25,17},{10,2},{18,10},{26,18},{... | collective-permute-start | bytes 1376264 | tf_op jit(solution)/shard_map/ppermute | solution.py:26
  70.7 4.0 %collective-permute-start = (bf16[128,1024]{1,0:T(8,128)(2,1)S(1)}, bf16[128,1024]{1,0:T(8,128)(2,1)S(1)}, u32[]{:S(2)}, u32[]{:S(2)}) collective-permute-start(bf16[128,1024]{1,0:T(8,128)(2,1)S(1)} %dynamic-slice_convert_fusion), channel_id=1, source_target_pairs={{0,2},{2,0},{4,6},{6,4},{1,3},{3,1},{5,7},{7,5},{8,10},{10,8},{12,... | collective-permute-start | bytes 786440 | tf_op jit(solution)/shard_map/ppermute | solution.py:20
Sparse Core Ops, SparseCore 0:
  48.6 20.8 reduce-scatter.1
where the time goes:
time: 83.7 us; the launch traced here: 83.2 us
  blocking collectives  26.1 us (31%)
  waiting for transfers between devices  14.6 us (17%)
  between operations  14.1 us (17%)
  local copies, waits for them, and re-layouts  12.3 us (15%)
  other arithmetic  10.8 us (13%)
  matrix products  3.97 us (5%)
  starting transfers between devices  1.4 us (2%)
    all_to_all x1, blocking collectives, on_device(): lax.all_to_all(slice_grad, 'tensor', split_axis=0, concat_axis=1, tiled=T...  26.1 us
    ppermute x1, waiting for transfers between devices, from_behind(): return lax.ppermute(array, axis, pairs)  12.2 us
    convert_element_type x2, local copies, waits for them, and re-layouts, on_device(): grad_w.astype(jnp.float32)  10.3 us
    convert_element_type x2, other arithmetic, on_device(): new_momentum = (momentum_decay * momentum[0, 0].astype(jnp.float32) + gra...  6.65 us
    dot_general x2, matrix products, contract(): lax.dot_general(left, right, (((0,), (0,)), ((), ())), preferred_element_...  3.97 us
    reduce_scatter x1, waiting for transfers between devices, on_device(): lax.psum_scatter(contract(columns, new_momentum).astype(jnp.bfloat16), 't...  2.43 us
    convert_element_type x1, other arithmetic, on_device(): grad_w.astype(jnp.float32)  2.03 us
  transfers between devices with their start and end apart: 3, of which 2 were waited for; matrix products, arithmetic and copies ran while one was open for 11% of the time, Pallas kernels for 0%

commit v1 on v0

v1 whole, which is shorter than its diff:
```python
import functools

import jax
import jax.numpy as jnp
from jax import lax
from jax.experimental import pallas as pl
from jax.experimental.pallas import tpu as pltpu
from jax.sharding import PartitionSpec as P

D = 3584
PANEL = 512
DECAY = 0.9
MESH = pl.DeviceIdType.MESH


def contract(left, right):
    return lax.dot_general(
        left, right, (((0,), (0,)), ((), ())), preferred_element_type=jnp.float32
    )


def kernel(
    sections, ranks,
    acts, hidden, counts, momentum, act_grad,
    new_momentum, gram, received,
    x_buf, g_own, m_buf, n_buf, xt_buf, g_in, panel,
    send1, recv1, send2, recv2, gram_buf, zero_buf,
    load_sem, store_sem, shift_send, shift_recv,
    g_send, g_recv, f_send, f_recv, s1_send, s1_recv, s2_send, s2_recv,
):
    section = lax.axis_index("pipe")
    expert_rank = lax.axis_index("expert")
    rank = lax.axis_index("tensor")
    pair = expert_rank // 2
    half = expert_rank % 2
    partner = {"expert": expert_rank + 1 - 2 * half}
    row_count, features = x_buf.shape
    rows, hidden_units = n_buf.shape
    width = g_own.shape[1]
    part = width // 2
    q = send1.shape[1]
    first, last = section == 0, section == sections - 1

    if features == rows:
        x_src = acts.at[0, 0, :, pl.ds(pl.multiple_of(rank * rows, 128), rows)]
    else:
        x_src = acts.at[0, 0]
    load_x = pltpu.make_async_copy(x_src, x_buf, load_sem.at[0])
    load_g = pltpu.make_async_copy(hidden.at[0, pair], g_own, load_sem.at[1])
    load_m = pltpu.make_async_copy(momentum.at[0, 0], m_buf, load_sem.at[2])
    load_x.start()
    load_g.start()
    load_m.start()

    barrier = pltpu.get_barrier_semaphore()
    pl.semaphore_signal(barrier, inc=1, device_id=partner, device_id_type=MESH)
    for k in range(1, ranks):
        pl.semaphore_signal(
            barrier, inc=1, device_id={"tensor": (rank + k) % ranks}, device_id_type=MESH
        )

    @pl.when(jnp.logical_not(first))
    def _():
        pl.semaphore_signal(barrier, inc=1, device_id={"pipe": section - 1}, device_id_type=MESH)

    @pl.when(jnp.logical_not(last))
    def _():
        pl.semaphore_signal(barrier, inc=1, device_id={"pipe": section + 1}, device_id_type=MESH)

    ends = jnp.where(first, 1, 0) + jnp.where(last, 1, 0)
    pl.semaphore_wait(barrier, ranks + 2 - ends)

    def send_share(peer):
        return pltpu.make_async_remote_copy(
            src_ref=hidden.at[0, pair, :, pl.ds(pl.multiple_of(half * part, 128), part)],
            dst_ref=g_in.at[rank, half],
            send_sem=g_send.at[peer],
            recv_sem=g_recv.at[rank],
            device_id={"tensor": peer},
            device_id_type=MESH,
        )

    def arrived_share(peer):
        return pltpu.make_async_remote_copy(
            src_ref=g_in.at[peer, half],
            dst_ref=g_in.at[peer, half],
            send_sem=g_send.at[peer],
            recv_sem=g_recv.at[peer],
            device_id={"tensor": peer},
            device_id_type=MESH,
        )

    def forward(peer, which):
        return pltpu.make_async_remote_copy(
            src_ref=g_in.at[peer, which],
            dst_ref=g_in.at[peer, which],
            send_sem=f_send.at[peer],
            recv_sem=f_recv.at[peer],
            device_id=partner,
            device_id_type=MESH,
        )

    peers = [(rank + k) % ranks for k in range(1, ranks)]
    for peer in peers:
        send_share(peer).start()

    shift = pltpu.make_async_remote_copy(
        src_ref=act_grad,
        dst_ref=received,
        send_sem=shift_send,
        recv_sem=shift_recv,
        device_id={"pipe": section - 1},
        device_id_type=MESH,
    )

    @pl.when(jnp.logical_not(first))
    def _():
        shift.start()

    load_x.wait()
    row = lax.broadcasted_iota(jnp.int32, (row_count, 1), 0)
    micro = counts.shape[2]
    block = row_count // micro
    limit = jnp.zeros((row_count, 1), jnp.int32)
    for b in range(micro):
        inside = jnp.logical_and(row >= b * block, row < (b + 1) * block)
        limit = jnp.where(inside, counts[0, pair, b] + b * block, limit)
    live = jnp.where(row < limit, 1.0, 0.0).astype(jnp.float32)
    masked = (x_buf[...].astype(jnp.float32) * live).astype(jnp.bfloat16)
    xt_buf[...] = masked.T

    def update(start, size, gradients):
        cols = pl.ds(pl.multiple_of(start, 128), size)
        if features == rows:
            x_rows = xt_buf[...]
        else:
            x_rows = xt_buf[pl.ds(pl.multiple_of(rank * rows, 16), rows), :]
        grad = jnp.dot(x_rows, gradients, preferred_element_type=jnp.float32)
        grad = grad.astype(jnp.bfloat16).astype(jnp.float32)
        n_buf[:, cols] = (DECAY * m_buf[:, cols].astype(jnp.float32) + grad).astype(jnp.bfloat16)

    load_g.wait()
    load_m.wait()
    update(rank * width, width, g_own[...])

    @pl.when(last)
    def _():
        zero_buf[...] = jnp.zeros_like(zero_buf)
        pltpu.make_async_copy(zero_buf, received, store_sem.at[2]).start()

    for peer in peers:
        arrived_share(peer).wait_recv()
        forward(peer, half).start()
        update(peer * width + half * part, part, g_in[peer, half])
    for peer in peers:
        forward(peer, 1 - half).wait_recv()
        update(peer * width + (1 - half) * part, part, g_in[peer, 1 - half])
    store_n = pltpu.make_async_copy(n_buf, new_momentum, store_sem.at[0])
    store_n.start()

    def pair_rows(owner):
        return pltpu.make_async_remote_copy(
            src_ref=send1.at[owner],
            dst_ref=recv1.at[owner],
            send_sem=s1_send.at[owner],
            recv_sem=s1_recv.at[owner],
            device_id=partner,
            device_id_type=MESH,
        )

    def rank_rows(peer, slot):
        return pltpu.make_async_remote_copy(
            src_ref=send2.at[peer],
            dst_ref=recv2.at[slot],
            send_sem=s2_send.at[peer],
            recv_sem=s2_recv.at[slot],
            device_id={"tensor": peer},
            device_id_type=MESH,
        )

    def own_half(owner):
        return panel[owner, pl.ds(pl.multiple_of(half * q, q), q), :]

    for owner in peers + [rank]:
        start = pl.multiple_of(owner * 2 * q, 128)
        panel[owner] = contract(n_buf[:, pl.ds(start, 2 * q)], n_buf[...])
        other = panel[owner, pl.ds(pl.multiple_of((1 - half) * q, q), q), :]
        send1[owner] = other.astype(jnp.bfloat16)
        pair_rows(owner).start()
    for owner in peers:
        pair_rows(owner).wait_recv()
        send2[owner] = (own_half(owner) + recv1[owner].astype(jnp.float32)).astype(jnp.bfloat16)
        rank_rows(owner, rank).start()
    pair_rows(rank).wait_recv()
    total = own_half(rank) + recv1[rank].astype(jnp.float32)
    for peer in peers:
        rank_rows(peer, peer).wait_recv()
        total = total + recv2[peer].astype(jnp.float32)
    gram_buf[...] = total / D
    store_gram = pltpu.make_async_copy(gram_buf, gram, store_sem.at[1])
    store_gram.start()

    for peer in peers:
        send_share(peer).wait_send()
        forward(peer, half).wait_send()
        rank_rows(peer, rank).wait_send()
    for owner in peers + [rank]:
        pair_rows(owner).wait_send()

    @pl.when(jnp.logical_not(first))
    def _():
        shift.wait_send()

    @pl.when(jnp.logical_not(last))
    def _():
        shift.wait_recv()

    @pl.when(last)
    def _():
        pltpu.make_async_copy(zero_buf, received, store_sem.at[2]).wait()

    store_n.wait()
    store_gram.wait()


def on_device(acts, hidden_grad, counts, momentum, act_grad):
    sections, ranks = lax.axis_size("pipe"), lax.axis_size("tensor")
    row_count, features = acts.shape[2:]
    rows, units = momentum.shape[2:]
    width = hidden_grad.shape[3]
    q = PANEL // (2 * ranks)
    x_cols = rows if rows % 128 == 0 else features
    bf16, f32 = jnp.bfloat16, jnp.float32
    dma = pltpu.SemaphoreType.DMA
    hbm = pl.BlockSpec(memory_space=pl.ANY)
    new_momentum, gram, received = pl.pallas_call(
        functools.partial(kernel, sections, ranks),
        out_shape=(
            jax.ShapeDtypeStruct((rows, units), bf16),
            jax.ShapeDtypeStruct((q, units), f32),
            jax.ShapeDtypeStruct(act_grad.shape, bf16),
        ),
        in_specs=[hbm, hbm, pl.BlockSpec(memory_space=pltpu.SMEM), hbm, hbm],
        out_specs=(hbm, hbm, hbm),
        scratch_shapes=[
            pltpu.VMEM((row_count, x_cols), bf16),
            pltpu.VMEM((row_count, width), bf16),
            pltpu.VMEM((rows, units), bf16),
            pltpu.VMEM((rows, units), bf16),
            pltpu.VMEM((x_cols, row_count), bf16),
            pltpu.VMEM((ranks, 2, row_count, width // 2), bf16),
            pltpu.VMEM((ranks, 2 * q, units), f32),
            pltpu.VMEM((ranks, q, units), bf16),
            pltpu.VMEM((ranks, q, units), bf16),
            pltpu.VMEM((ranks, q, units), bf16),
            pltpu.VMEM((ranks, q, units), bf16),
            pltpu.VMEM((q, units), f32),
            pltpu.VMEM(act_grad.shape, bf16),
            dma((3,)), dma((3,)), dma, dma,
            dma((ranks,)), dma((ranks,)), dma((ranks,)), dma((ranks,)),
            dma((ranks,)), dma((ranks,)), dma((ranks,)), dma((ranks,)),
        ],
        compiler_params=pltpu.CompilerParams(
            collective_id=0, has_side_effects=True, vmem_limit_bytes=60 * 2**20
        ),
    )(acts, hidden_grad, counts, momentum, act_grad)
    return (new_momentum[None, None], gram[None, None], received)


def solution(mesh):
    return jax.shard_map(
        on_device,
        mesh=mesh,
        in_specs=(
            P("pipe", "expert", None, None),
            P("pipe", None, None, "tensor"),
            P("pipe", None, None),
            P("pipe", "expert", "tensor", None),
            P("pipe", "expert", "tensor"),
        ),
        out_specs=(
            P("pipe", "expert", "tensor", None),
            P("pipe", "expert", "tensor", None),
            P("pipe", "expert", "tensor"),
        ),
        check_vma=False,
    )
```

time: 83.7 us -> 25.5 us (0.30)
  blocking collectives: 26.1 us -> 0 us
  Pallas kernels: 0 us -> 20.1 us
  waiting for transfers between devices: 14.6 us -> 0 us
  between operations: 14.1 us -> 0.66 us
  other arithmetic: 10.8 us -> 0 us
  local copies, waits for them, and re-layouts: 12.3 us -> 4.52 us
  matrix products: 3.97 us -> 0 us
  starting transfers between devices: 1.4 us -> 0 us
    all_to_all x1 -> x0, blocking collectives: 26.1 us -> none  [on_device(): lax.all_to_all(slice_grad, 'tensor', split_axis=0, concat_axis=1, tiled=T...]
    pallas_call x0 -> x1, Pallas kernels: none -> 20.1 us  [on_device(): pl.pallas_call(functools.partial(kernel, sections, ranks), out_shape=(jax...]
    ppermute x2 -> x0, waiting for transfers between devices: 12.2 us -> none  [the longest x1 12.2 us: from_behind(): return lax.ppermute(array, axis, pairs)]
    convert_element_type x3 -> x0, local copies, waits for them, and re-layouts: 10.3 us -> none  [the longest x2 10.3 us: on_device(): grad_w.astype(jnp.float32)]
    convert_element_type x4 -> x0, other arithmetic: 9.82 us -> none  [the longest x2 6.65 us: on_device(): new_momentum = (momentum_decay * momentum[0, 0].astype(jnp.float32) + gra...]
    dot_general x2 -> x0, matrix products: 3.97 us -> none  [contract(): lax.dot_general(left, right, (((0,), (0,)), ((), ())), preferred_element_...]
    unnamed x5 -> x7, local copies, waits for them, and re-layouts: 1.07 us -> 4.52 us
    reduce_scatter x1 -> x0, waiting for transfers between devices: 2.43 us -> none  [on_device(): lax.psum_scatter(contract(columns, new_momentum).astype(jnp.bfloat16), 't...]
  transfers between devices with their start and end apart: 3 -> 0, of which waited for: 2 -> 0; matrix products, arithmetic and copies ran while one was open for 11% -> 0% of each run, Pallas kernels for 0% -> 0%
where the time goes in v1:
time: 25.5 us; the launch traced here: 25.3 us
  Pallas kernels  20.1 us (79%)
  local copies, waits for them, and re-layouts  4.52 us (18%)
  between operations  0.66 us (3%)
    pallas_call x1, Pallas kernels, on_device(): pl.pallas_call(functools.partial(kernel, sections, ranks), out_shape=(jax...  20.1 us
    unnamed x7, local copies, waits for them, and re-layouts  4.52 us

profile of v1, /device:TPU:0, one launch (start us, length us, event | category | flops | bytes accessed | tf_op | source)
XLA Modules:
  0.0 25.3 jit_solution(16296728987082105568)
XLA Ops:
  0.6 20.1 %shard_map.76 = (bf16[896,1024]{1,0:T(8,128)(2,1)}, f32[128,1024]{1,0:T(8,128)}, bf16[1,64,3584]{2,1,0:T(8,128)(2,1)}) custom-call(bf16[1,1,256,1792]{3,2,1,0:T(8,128)(2,1)} %acts.1, bf16[1,2,256,512]{3,2,1,0:T(8,128)(2,1)} %hidden.1, s32[1,2,2]{2,1,0:T(2,128)} %counts.1, bf16[1,1,896,1024]{3,2,1,0:T(8,128)(2,1)} %momentum.1, bf16[1,64,3584]{2,1,0:T(8,128)(2,1)} %act_grad.1), custom_call_target="tpu_custom_call" | custom-call | tf_op jit(solution)/shard_map/pallas_call | solution.py:236
  20.8 0.0 copy-start
  20.8 0.0 copy-start.1
  20.8 3.0 %copy.11 = bf16[1,1,896,1024]{3,2,1,0:T(8,128)(2,1)} copy(bf16[1,1,896,1024]{3,2,1,0:T(8,128)(2,1)} %bitcast.2) | data formatting | bytes 3670016
  23.7 0.0 copy-done
  23.7 0.8 %copy.12 = f32[1,1,128,1024]{3,2,1,0:T(8,128)} copy(f32[1,1,128,1024]{3,2,1,0:T(8,128)S(1)} %bitcast.3) | data formatting | bytes 1048576
  24.5 0.0 copy-done.1
  24.5 0.8 %copy.13 = bf16[1,64,3584]{2,1,0:T(8,128)(2,1)} copy(bf16[1,64,3584]{2,1,0:T(8,128)(2,1)S(1)} %copy-done.1) | data formatting | bytes 917504
Async XLA Ops:
  20.8 3.0 %copy-start = (f32[128,1024]{1,0:T(8,128)S(1)}, f32[128,1024]{1,0:T(8,128)}, u32[]{:S(2)}) copy-start(f32[128,1024]{1,0:T(8,128)} %get-tuple-element.7) | copy-start | bytes 1572868
  20.8 3.8 %copy-start.1 = (bf16[1,64,3584]{2,1,0:T(8,128)(2,1)S(1)}, bf16[1,64,3584]{2,1,0:T(8,128)(2,1)}, u32[]{:S(2)}) copy-start(bf16[1,64,3584]{2,1,0:T(8,128)(2,1)} %get-tuple-element.14) | copy-start | bytes 1376260

commit v2 on v0

v2 whole, which is shorter than its diff:
```python
import functools

import jax
import jax.numpy as jnp
from jax import lax
from jax.experimental import pallas as pl
from jax.experimental.pallas import tpu as pltpu
from jax.sharding import PartitionSpec as P

D = 3584
PANEL = 512
DECAY = 0.9
MESH = pl.DeviceIdType.MESH


def kernel(
    sections, ranks,
    acts, hidden, counts, momentum, act_grad,
    new_momentum, gram, received,
    x_buf, g_own, m_buf, xt_buf, g_in, nt_buf, own, send1, recv1, send2, recv2,
    load_sem, shift_send, shift_recv,
    g_send, g_recv, f_send, f_recv, s1_send, s1_recv, s2_send, s2_recv,
):
    section = lax.axis_index("pipe")
    expert_rank = lax.axis_index("expert")
    rank = lax.axis_index("tensor")
    pair = expert_rank // 2
    half = expert_rank % 2
    partner = {"expert": expert_rank + 1 - 2 * half}
    row_count, features = x_buf.shape
    rows, hidden_units = new_momentum.shape
    q, wide = send1.shape[2:]
    per_rank = g_own.shape[1] // wide
    share = row_count // 2
    first, last = section == 0, section == sections - 1

    if features == rows:
        x_src = acts.at[0, 0, :, pl.ds(pl.multiple_of(rank * rows, 128), rows)]
    else:
        x_src = acts.at[0, 0]
    load_x = pltpu.make_async_copy(x_src, x_buf, load_sem.at[0])
    load_g = pltpu.make_async_copy(hidden.at[0, pair], g_own, load_sem.at[1])
    load_m = pltpu.make_async_copy(momentum.at[0, 0], m_buf, load_sem.at[2])
    load_x.start()
    load_g.start()
    load_m.start()

    barrier = pltpu.get_barrier_semaphore()
    pl.semaphore_signal(barrier, inc=1, device_id=partner, device_id_type=MESH)
    for k in range(1, ranks):
        pl.semaphore_signal(
            barrier, inc=1, device_id={"tensor": (rank + k) % ranks}, device_id_type=MESH
        )

    @pl.when(jnp.logical_not(first))
    def _():
        pl.semaphore_signal(barrier, inc=1, device_id={"pipe": section - 1}, device_id_type=MESH)

    @pl.when(jnp.logical_not(last))
    def _():
        pl.semaphore_signal(barrier, inc=1, device_id={"pipe": section + 1}, device_id_type=MESH)

    ends = jnp.where(first, 1, 0) + jnp.where(last, 1, 0)
    pl.semaphore_wait(barrier, ranks + 2 - ends)

    shift = pltpu.make_async_remote_copy(
        src_ref=act_grad,
        dst_ref=received,
        send_sem=shift_send,
        recv_sem=shift_recv,
        device_id={"pipe": section - 1},
        device_id_type=MESH,
    )

    def clear_dead_rows():
        row = lax.broadcasted_iota(jnp.int32, (row_count, 1), 0)
        micro = counts.shape[2]
        block = row_count // micro
        limit = jnp.zeros((row_count, 1), jnp.int32)
        for b in range(micro):
            inside = jnp.logical_and(row >= b * block, row < (b + 1) * block)
            limit = jnp.where(inside, counts[0, pair, b] + b * block, limit)
        live = jnp.where(row < limit, 1.0, 0.0).astype(jnp.float32)
        masked = (x_buf[...].astype(jnp.float32) * live).astype(jnp.bfloat16)
        xt_buf[...] = masked.T

    def own_share(which):
        return pl.ds(pl.multiple_of(which * share, share), share)

    def as_rank(me):
        peers = [(me + k) % ranks for k in range(1, ranks)]

        def send_share(peer, c):
            return pltpu.make_async_remote_copy(
                src_ref=hidden.at[0, pair, own_share(half), pl.ds(c * wide, wide)],
                dst_ref=g_in.at[me, c, own_share(half)],
                send_sem=g_send.at[peer, c],
                recv_sem=g_recv.at[me, c],
                device_id={"tensor": peer},
                device_id_type=MESH,
            )

        def arrived_share(peer, c):
            place = g_in.at[peer, c, own_share(half)]
            return pltpu.make_async_remote_copy(
                src_ref=place,
                dst_ref=place,
                send_sem=g_send.at[peer, c],
                recv_sem=g_recv.at[peer, c],
                device_id={"tensor": peer},
                device_id_type=MESH,
            )

        def forward(peer, c, which):
            place = g_in.at[peer, c, own_share(which)]
            return pltpu.make_async_remote_copy(
                src_ref=place,
                dst_ref=place,
                send_sem=f_send.at[peer, c],
                recv_sem=f_recv.at[peer, c],
                device_id=partner,
                device_id_type=MESH,
            )

        def to_partner(owner, j):
            return pltpu.make_async_remote_copy(
                src_ref=send1.at[owner, j],
                dst_ref=recv1.at[owner, j],
                send_sem=s1_send.at[owner, j],
                recv_sem=s1_recv.at[owner, j],
                device_id=partner,
                device_id_type=MESH,
            )

        def to_rank(peer, slot, j):
            return pltpu.make_async_remote_copy(
                src_ref=send2.at[peer, j],
                dst_ref=recv2.at[slot, j],
                send_sem=s2_send.at[peer, j],
                recv_sem=s2_recv.at[slot, j],
                device_id={"tensor": peer},
                device_id_type=MESH,
            )

        for c in range(per_rank):
            for peer in peers:
                send_share(peer, c).start()

        @pl.when(jnp.logical_not(first))
        def _():
            shift.start()

        load_x.wait()
        clear_dead_rows()
        load_g.wait()
        load_m.wait()

        def update(j, gradients):
            cols = pl.ds(j * wide, wide)
            if features == rows:
                x_rows = xt_buf[...]
            else:
                x_rows = xt_buf[pl.ds(me * rows, rows), :]
            grad = jnp.dot(x_rows, gradients, preferred_element_type=jnp.float32)
            grad = grad.astype(jnp.bfloat16).astype(jnp.float32)
            new = (DECAY * m_buf[:, cols].astype(jnp.float32) + grad).astype(jnp.bfloat16)
            new_momentum[:, cols] = new
            if j < ranks:
                nt_buf[j] = new.T

        def piece(owner, j):
            sums = jnp.dot(
                nt_buf[owner],
                new_momentum[:, pl.ds(j * wide, wide)],
                preferred_element_type=jnp.float32,
            )
            top, bottom = sums[:q], sums[q:]
            own[owner, j] = jnp.where(half == 0, top, bottom)
            send1[owner, j] = jnp.where(half == 0, bottom, top).astype(jnp.bfloat16)
            to_partner(owner, j).start()

        def pass_on(owner, j):
            to_partner(owner, j).wait_recv()
            both = own[owner, j] + recv1[owner, j].astype(jnp.float32)
            send2[owner, j] = both.astype(jnp.bfloat16)
            to_rank(owner, me, j).start()

        ready, waiting = [], []

        def pieces(new):
            ready.extend(new)
            for owner in peers + [me]:
                if owner in ready:
                    for j in ready if owner in new else new:
                        piece(owner, j)
                        if owner != me:
                            waiting.append((owner, j))

        mine = [me * per_rank + c for c in range(per_rank)]
        for c in range(per_rank):
            update(mine[c], g_own[:, c * wide:(c + 1) * wide])
        pieces(mine)

        @pl.when(last)
        def _():
            received[...] = jnp.zeros_like(received)

        arrivals = [(peer, c) for c in range(per_rank) for peer in peers]
        for peer, c in arrivals:
            arrived_share(peer, c).wait_recv()
            forward(peer, c, half).start()
            while waiting:
                pass_on(*waiting.pop(0))
            forward(peer, c, 1 - half).wait_recv()
            update(peer * per_rank + c, g_in[peer, c])
            pieces([peer * per_rank + c])
        while waiting:
            pass_on(*waiting.pop(0))

        order = ready
        for j in order:
            to_partner(me, j).wait_recv()
            own[me, j] = own[me, j] + recv1[me, j].astype(jnp.float32)
        for j in order[per_rank:] + order[:per_rank]:
            total = own[me, j]
            for peer in peers:
                to_rank(peer, peer, j).wait_recv()
                total = total + recv2[peer, j].astype(jnp.float32)
            gram[:, pl.ds(j * wide, wide)] = total / D

        for peer, c in arrivals:
            send_share(peer, c).wait_send()
            forward(peer, c, half).wait_send()
        for j in order:
            for owner in peers + [me]:
                to_partner(owner, j).wait_send()
            for peer in peers:
                to_rank(peer, me, j).wait_send()

    for me in range(ranks):

        @pl.when(rank == me)
        def _():
            as_rank(me)

    @pl.when(jnp.logical_not(first))
    def _():
        shift.wait_send()

    @pl.when(jnp.logical_not(last))
    def _():
        shift.wait_recv()


def write_out(*refs):
    count = len(refs) // 2
    sems = refs[-1]
    copies = [
        pltpu.make_async_copy(refs[i], refs[count + i], sems.at[i]) for i in range(count)
    ]
    for copy in copies:
        copy.start()
    for copy in copies:
        copy.wait()


def on_device(acts, hidden_grad, counts, momentum, act_grad):
    sections, ranks = lax.axis_size("pipe"), lax.axis_size("tensor")
    row_count, features = acts.shape[2:]
    rows, units = momentum.shape[2:]
    width = hidden_grad.shape[3]
    q = PANEL // (2 * ranks)
    wide = 2 * q
    blocks = units // wide
    x_cols = rows if rows % 128 == 0 else features
    bf16, f32 = jnp.bfloat16, jnp.float32
    vmem, dma = pltpu.VMEM, pltpu.SemaphoreType.DMA
    hbm = pl.BlockSpec(memory_space=pltpu.HBM)
    anywhere = pl.BlockSpec(memory_space=pl.ANY)
    in_vmem = pl.BlockSpec(memory_space=vmem)

    def keep(x):
        return pltpu.with_memory_space_constraint(x, pltpu.HBM)

    results = pl.pallas_call(
        functools.partial(kernel, sections, ranks),
        out_shape=(
            vmem((rows, units), bf16),
            vmem((q, units), f32),
            vmem(act_grad.shape, bf16),
        ),
        in_specs=[hbm, hbm, pl.BlockSpec(memory_space=pltpu.SMEM), hbm, hbm],
        out_specs=(in_vmem, in_vmem, in_vmem),
        scratch_shapes=[
            vmem((row_count, x_cols), bf16),
            vmem((row_count, width), bf16),
            vmem((rows, units), bf16),
            vmem((x_cols, row_count), bf16),
            vmem((ranks, width // wide, row_count, wide), bf16),
            vmem((ranks, wide, rows), bf16),
            vmem((ranks, blocks, q, wide), f32),
            vmem((ranks, blocks, q, wide), bf16),
            vmem((ranks, blocks, q, wide), bf16),
            vmem((ranks, blocks, q, wide), bf16),
            vmem((ranks, blocks, q, wide), bf16),
            dma((3,)), dma, dma,
            dma((ranks, width // wide)), dma((ranks, width // wide)),
            dma((ranks, width // wide)), dma((ranks, width // wide)),
            dma((ranks, blocks)), dma((ranks, blocks)),
            dma((ranks, blocks)), dma((ranks, blocks)),
        ],
        compiler_params=pltpu.CompilerParams(
            collective_id=0, has_side_effects=True, vmem_limit_bytes=32 * 2**20
        ),
    )(keep(acts), keep(hidden_grad), keep(counts), keep(momentum), keep(act_grad))
    new_momentum, gram, received = pl.pallas_call(
        write_out,
        out_shape=tuple(pltpu.HBM(r.shape, r.dtype) for r in results),
        in_specs=[in_vmem] * 3,
        out_specs=(hbm,) * 3,
        scratch_shapes=[dma((3,))],
    )(*[pltpu.with_memory_space_constraint(r, vmem) for r in results])
    return (new_momentum[None, None], gram[None, None], received)


def solution(mesh):
    return jax.shard_map(
        on_device,
        mesh=mesh,
        in_specs=(
            P("pipe", "expert", None, None),
            P("pipe", None, None, "tensor"),
            P("pipe", None, None),
            P("pipe", "expert", "tensor", None),
            P("pipe", "expert", "tensor"),
        ),
        out_specs=(
            P("pipe", "expert", "tensor", None),
            P("pipe", "expert", "tensor", None),
            P("pipe", "expert", "tensor"),
        ),
        check_vma=False,
    )
```

time: 83.7 us -> 20.6 us (0.25)
  blocking collectives: 26.1 us -> 0 us
  Pallas kernels: 0 us -> 19.8 us
  waiting for transfers between devices: 14.6 us -> 0 us
  between operations: 14.1 us -> 0.64 us
  local copies, waits for them, and re-layouts: 12.3 us -> 0 us
  other arithmetic: 10.8 us -> 0 us
  matrix products: 3.97 us -> 0 us
  starting transfers between devices: 1.4 us -> 0 us
    all_to_all x1 -> x0, blocking collectives: 26.1 us -> none  [on_device(): lax.all_to_all(slice_grad, 'tensor', split_axis=0, concat_axis=1, tiled=T...]
    pallas_call x0 -> x2, Pallas kernels: none -> 19.8 us  [the longest x1 18.3 us: on_device(): pl.pallas_call(functools.partial(kernel, sections, ranks), out_shape=(vme...]
    ppermute x2 -> x0, waiting for transfers between devices: 12.2 us -> none  [the longest x1 12.2 us: from_behind(): return lax.ppermute(array, axis, pairs)]
    convert_element_type x3 -> x0, local copies, waits for them, and re-layouts: 10.3 us -> none  [the longest x2 10.3 us: on_device(): grad_w.astype(jnp.float32)]
    convert_element_type x4 -> x0, other arithmetic: 9.82 us -> none  [the longest x2 6.65 us: on_device(): new_momentum = (momentum_decay * momentum[0, 0].astype(jnp.float32) + gra...]
    dot_general x2 -> x0, matrix products: 3.97 us -> none  [contract(): lax.dot_general(left, right, (((0,), (0,)), ((), ())), preferred_element_...]
    reduce_scatter x1 -> x0, waiting for transfers between devices: 2.43 us -> none  [on_device(): lax.psum_scatter(contract(columns, new_momentum).astype(jnp.bfloat16), 't...]
    ppermute x2 -> x0, starting transfers between devices: 1.36 us -> none  [the longest x1 1.29 us: from_behind(): return lax.ppermute(array, axis, pairs)]
  transfers between devices with their start and end apart: 3 -> 0, of which waited for: 2 -> 0; matrix products, arithmetic and copies ran while one was open for 11% -> 0% of each run, Pallas kernels for 0% -> 0%
where the time goes in v2:
time: 20.6 us; the launch traced here: 20.5 us
  Pallas kernels  19.8 us (96%)
  between operations  0.64 us (3%)
    pallas_call x1, Pallas kernels, on_device(): pl.pallas_call(functools.partial(kernel, sections, ranks), out_shape=(vme...  18.3 us
    pallas_call x1, Pallas kernels, on_device(): pl.pallas_call(write_out, out_shape=tuple((pltpu.HBM(r.shape, r.dtype) fo...  1.57 us

profile of v2, /device:TPU:0, one launch (start us, length us, event | category | flops | bytes accessed | tf_op | source)
XLA Modules:
  0.0 20.5 jit_solution(10140233937664030219)
XLA Ops:
  0.6 18.3 %shard_map.76 = (bf16[896,1024]{1,0:T(8,128)(2,1)S(1)}, f32[128,1024]{1,0:T(8,128)S(1)}, bf16[1,64,3584]{2,1,0:T(8,128)(2,1)S(1)}) custom-call(bf16[1,1,256,1792]{3,2,1,0:T(8,128)(2,1)} %acts.1, bf16[1,2,256,512]{3,2,1,0:T(8,128)(2,1)} %hidden.1, s32[1,2,2]{2,1,0:T(2,128)} %counts.1, bf16[1,1,896,1024]{3,2,1,0:T(8,128)(2,1)} %momentum.1, ...), custom_call_target="tpu_custom_call" | custom-call | tf_op jit(solution)/shard_map/pallas_call | solution.py:285
  18.9 1.6 %shard_map.77 = (bf16[896,1024]{1,0:T(8,128)(2,1)}, f32[128,1024]{1,0:T(8,128)}, bf16[1,64,3584]{2,1,0:T(8,128)(2,1)}) custom-call(bf16[896,1024]{1,0:T(8,128)(2,1)S(1)} %get-tuple-element.9.refs_0_, f32[128,1024]{1,0:T(8,128)S(1)} %get-tuple-element.10.refs_1_, bf16[1,64,3584]{2,1,0:T(8,128)(2,1)S(1)} %get-tuple-element.11.refs_2_), custom_call_target="tpu_custom_call" | custom-call | tf_op jit(solution)/shard_map/pallas_call | solution.py:316
